TPU v7x, 512 devices: a whole 4x4x16 slice. The times are simulated.
512 devices in a mesh: gy: 16 (over x, z_lo), gx: 32 (over y, z_hi, core).
Axes of the slice: x: 4, y: 4, z: 16 (z_hi: 4, z_lo: 4; z = z_hi * 4 + z_lo), core: 2. Of those that a mesh axis runs over, the one named last changes fastest.
Arguments:
- field: bfloat16 [256, 256, 1024], P('gx', 'gy'), may hold values from -6 to 6
- center_block: bfloat16 [64, 64], replicated, may hold values from -0.75 to 0.75
- couple_blocks: bfloat16 [6, 64, 64], replicated, may hold values from -0.75 to 0.75
- cell_index: int32 [16, 32, 32, 32], P('gy', 'gx'), may hold values from 0 to 2047, as said below
- slot_counts: int32 [16, 32, 32], P('gy', 'gx'), may hold values from 0 to 32, as said below
- assays: bfloat16 [16, 32, 32, 2048], P('gy', 'gx'), may hold values from -6 to 6
- assay_weights: bfloat16 [16, 32, 32, 2048], P('gy', 'gx'), may hold values from 0.5 to 4
Outputs:
- gradient: bfloat16 [256, 256, 1024], P('gx', 'gy')
Inputs may be any that keep to these rules, and one draw needn't show every extreme that they name: `cell_index`: local cell numbers within the destination tile, every slot holds a valid one. `slot_counts`: composites of a list; some list is full, and some tile receives full lists from every owner of its band.
All inputs are finite; a program needn't handle non-finite values.
Results may differ from a plain program's by a relative error of at most 0.0039.
Values may be sent and summed in bfloat16 or wider, within the bound.
A program may use at most 64 MiB of HBM per device.

v0:
```python
import jax
import jax.numpy as jnp
from jax import lax
from jax.sharding import PartitionSpec as P


def with_halo(block, sides, width):
    for axis, dim in sides:
        count = lax.axis_size(axis)
        forward = [(i, i + 1) for i in range(count - 1)]
        backward = [(target, source) for source, target in forward]
        low = lax.ppermute(
            lax.slice_in_dim(block, block.shape[dim] - width, None, axis=dim), axis, forward
        )
        high = lax.ppermute(lax.slice_in_dim(block, 0, width, axis=dim), axis, backward)
        block = jnp.concatenate([low, block, high], axis=dim)
    return block


def spread(block, center, couple, form, flip):
    padded = jnp.pad(block, ((0, 0), (0, 0), (1, 1), (0, 0)))
    middle = padded[1:-1, 1:-1, 1:-1]
    plus_x, minus_x = (padded[2:, 1:-1, 1:-1], padded[:-2, 1:-1, 1:-1])
    plus_y, minus_y = (padded[1:-1, 2:, 1:-1], padded[1:-1, :-2, 1:-1])
    plus_z, minus_z = (padded[1:-1, 1:-1, 2:], padded[1:-1, 1:-1, :-2])
    if flip:
        nearby = (minus_x, plus_x, minus_y, plus_y, minus_z, plus_z)
    else:
        nearby = (plus_x, minus_x, plus_y, minus_y, plus_z, minus_z)
    total = jnp.einsum(form, middle, center, preferred_element_type=jnp.float32)
    for which in range(6):
        total = total - jnp.einsum(
            form, nearby[which], couple[which], preferred_element_type=jnp.float32
        )
    return total


def widen(values):
    return with_halo(values, (("gy", 1), ("gx", 0)), 1)


def on_device(field, center_block, couple_blocks, cell_index, slot_counts, assays, assay_weights):
    rows_x, rows_y, merged = field.shape
    elems = center_block.shape[0]
    thick = merged // elems
    slots = cell_index.shape[-1]
    tiles = lax.axis_size("gx")
    first = widen(field).reshape(rows_x + 2, rows_y + 2, thick, elems)
    image = spread(first, center_block, couple_blocks, "xyze,ef->xyzf", False).astype(jnp.bfloat16)
    second = widen(image.reshape(rows_x, rows_y, merged)).reshape(
        rows_x + 2, rows_y + 2, thick, elems
    )
    prior = spread(second, center_block, couple_blocks, "xyze,fe->xyzf", True)
    cell_rows = field.reshape(rows_x * rows_y * thick, elems)
    own_index = cell_index.reshape(tiles, slots)
    own_counts = slot_counts.reshape(tiles)
    own_assays = assays.reshape(tiles, slots * elems)
    own_weights = assay_weights.reshape(tiles, slots * elems)
    slot_ids = jnp.arange(slots, dtype=jnp.int32)[None, :]
    got_index = lax.all_to_all(own_index, "gx", split_axis=0, concat_axis=0, tiled=True)
    fetched = cell_rows[got_index].reshape(tiles, slots * elems)
    returned = lax.all_to_all(fetched, "gx", split_axis=0, concat_axis=0, tiled=True)
    values = returned.reshape(tiles, slots, elems).astype(jnp.float32)
    target = own_assays.reshape(tiles, slots, elems).astype(jnp.float32)
    scale = own_weights.reshape(tiles, slots, elems).astype(jnp.float32)
    used = slot_ids < own_counts[:, None]
    misfit = jnp.where(used[:, :, None], scale * (target - values), jnp.float32(0.0))
    arrived = (
        lax.all_to_all(
            misfit.reshape(tiles, slots * elems).astype(jnp.bfloat16),
            "gx",
            split_axis=0,
            concat_axis=0,
            tiled=True,
        )
        .astype(jnp.float32)
        .reshape(tiles, slots, elems)
    )
    data = (
        jnp.zeros((rows_x * rows_y * thick, elems), jnp.float32)
        .at[got_index.reshape(-1)]
        .add(arrived.reshape(-1, elems))
    )
    total = data.reshape(rows_x, rows_y, thick, elems) - prior
    return total.astype(jnp.bfloat16).reshape(rows_x, rows_y, merged)


def solution(mesh):
    in_specs = (
        P("gx", "gy", None),
        P(),
        P(),
        P("gy", "gx", None, None),
        P("gy", "gx", None),
        P("gy", "gx", None, None),
        P("gy", "gx", None, None),
    )
    out_specs = P("gx", "gy", None)
    return jax.shard_map(
        on_device, mesh=mesh, in_specs=in_specs, out_specs=out_specs, check_vma=False
    )
```

profile of v0, /device:TPU:3, one launch (start us, length us, event | category | flops | bytes accessed | tf_op | source)
XLA Modules:
  0.0 139.8 jit_solution(14040250647073293801)
XLA Ops:
  0.0 18.7 %all-to-all-start = ((s32[32,1,32]{2,1,0:T(1,128)}), s32[32,1,32]{2,1,0:T(1,128)S(1)}, u32[]{:S(2)}, u32[]{:S(2)}) async-start(s32[32,1,32]{2,1,0:T(1,128)} %bitcast.90), calls=%async_computation | async-start | bytes 32768 | tf_op jit(solution)/shard_map/all_to_all | solution.py:60
  18.7 1.0 fusion.61
  19.7 2.6 %collective-permute-start = (bf16[8,1,1024]{2,1,0:T(2,128)(2,1)S(1)}, bf16[8,1,1024]{2,1,0:T(2,128)(2,1)S(1)}, u32[]{:S(2)}, u32[]{:S(2)}) collective-permute-start(bf16[8,1,1024]{2,1,0:T(2,128)(2,1)S(1)} %get-tuple-element.11), channel_id=1, source_target_pairs={{0,32},{32,64},{64,96},{96,128},{128,160},{160,192},{192,224},{224... | collective-permute-start | bytes 49160 | tf_op jit(solution)/shard_map/ppermute | solution.py:12
  22.4 5.3 %collective-permute-start.1 = (bf16[8,1,1024]{2,1,0:T(2,128)(2,1)S(1)}, bf16[8,1,1024]{2,1,0:T(2,128)(2,1)S(1)}, u32[]{:S(2)}, u32[]{:S(2)}) collective-permute-start(bf16[8,1,1024]{2,1,0:T(2,128)(2,1)S(1)} %get-tuple-element.12), channel_id=1, source_target_pairs={{32,0},{64,32},{96,64},{128,96},{160,128},{192,160},{224,192},{256... | collective-permute-start | bytes 49160 | tf_op jit(solution)/shard_map/ppermute | solution.py:15
  27.7 0.7 iota_compare_fusion
  28.5 1.3 reshape.146
  30.0 0.2 broadcast_in_dim.23
  30.3 8.0 %collective-permute-start.2 = (bf16[1,18,1024]{2,1,0:T(8,128)(2,1)S(1)}, bf16[1,18,1024]{2,1,0:T(8,128)(2,1)S(1)}, u32[]{:S(2)}, u32[]{:S(2)}) collective-permute-start(bf16[1,18,1024]{2,1,0:T(8,128)(2,1)S(1)} %get-tuple-element.7), channel_id=1, source_target_pairs={{0,1},{1,2},{2,3},{3,4},{4,5},{5,6},{6,7},{7,8},{8,9},{9,10},{10,1... | collective-permute-start | bytes 110600 | tf_op jit(solution)/shard_map/ppermute | solution.py:12
  38.3 1.9 %collective-permute-start.3 = (bf16[1,18,1024]{2,1,0:T(8,128)(2,1)S(1)}, bf16[1,18,1024]{2,1,0:T(8,128)(2,1)S(1)}, u32[]{:S(2)}, u32[]{:S(2)}) collective-permute-start(bf16[1,18,1024]{2,1,0:T(8,128)(2,1)S(1)} %get-tuple-element.8), channel_id=1, source_target_pairs={{1,0},{2,1},{3,2},{4,3},{5,4},{6,5},{7,6},{8,7},{9,8},{10,9},{11,1... | collective-permute-start | bytes 110600 | tf_op jit(solution)/shard_map/ppermute | solution.py:15
  40.3 0.5 broadcast.56
  40.8 0.7 reduce.5
  41.6 6.1 %collective-permute-done.3 = bf16[1,18,1024]{2,1,0:T(8,128)(2,1)S(1)} collective-permute-done((bf16[1,18,1024]{2,1,0:T(8,128)(2,1)S(1)}, bf16[1,18,1024]{2,1,0:T(8,128)(2,1)S(1)}, u32[]{:S(2)}, u32[]{:S(2)}) %collective-permute-start.3) | collective-permute-done | bytes 36896 | tf_op jit(solution)/shard_map/ppermute | solution.py:15
  47.8 0.5 reshape.148
  48.3 0.3 fusion.14
  48.6 0.3 fusion.13
  48.9 0.3 fusion.30
  49.2 0.3 fusion.34
  49.5 0.3 fusion.38
  49.7 0.3 fusion.42
  50.0 0.5 fusion.11
  50.5 0.3 reshape.149
  50.9 1.9 %collective-permute-start.4 = (bf16[8,1,1024]{2,1,0:T(2,128)(2,1)S(1)}, bf16[8,1,1024]{2,1,0:T(2,128)(2,1)S(1)}, u32[]{:S(2)}, u32[]{:S(2)}) collective-permute-start(bf16[8,1,1024]{2,1,0:T(2,128)(2,1)S(1)} %get-tuple-element.9), channel_id=1, source_target_pairs={{0,32},{32,64},{64,96},{96,128},{128,160},{160,192},{192,224},{224... | collective-permute-start | bytes 49160 | tf_op jit(solution)/shard_map/ppermute | solution.py:12
  52.8 6.1 %collective-permute-start.5 = (bf16[8,1,1024]{2,1,0:T(2,128)(2,1)S(1)}, bf16[8,1,1024]{2,1,0:T(2,128)(2,1)S(1)}, u32[]{:S(2)}, u32[]{:S(2)}) collective-permute-start(bf16[8,1,1024]{2,1,0:T(2,128)(2,1)S(1)} %get-tuple-element.10), channel_id=1, source_target_pairs={{32,0},{64,32},{96,64},{128,96},{160,128},{192,160},{224,192},{256... | collective-permute-start | bytes 49160 | tf_op jit(solution)/shard_map/ppermute | solution.py:15
  59.0 0.9 collective-permute-done.5
  59.9 3.0 %collective-permute-start.6 = (bf16[1,18,1024]{2,1,0:T(8,128)(2,1)S(1)}, bf16[1,18,1024]{2,1,0:T(8,128)(2,1)S(1)}, u32[]{:S(2)}, u32[]{:S(2)}) collective-permute-start(bf16[1,18,1024]{2,1,0:T(8,128)(2,1)S(1)} %get-tuple-element.5), channel_id=1, source_target_pairs={{0,1},{1,2},{2,3},{3,4},{4,5},{5,6},{6,7},{7,8},{8,9},{9,10},{10,1... | collective-permute-start | bytes 110600 | tf_op jit(solution)/shard_map/ppermute | solution.py:12
  63.0 1.9 %collective-permute-start.7 = (bf16[1,18,1024]{2,1,0:T(8,128)(2,1)S(1)}, bf16[1,18,1024]{2,1,0:T(8,128)(2,1)S(1)}, u32[]{:S(2)}, u32[]{:S(2)}) collective-permute-start(bf16[1,18,1024]{2,1,0:T(8,128)(2,1)S(1)} %get-tuple-element.6), channel_id=1, source_target_pairs={{1,0},{2,1},{3,2},{4,3},{5,4},{6,5},{7,6},{8,7},{9,8},{10,9},{11,1... | collective-permute-start | bytes 110600 | tf_op jit(solution)/shard_map/ppermute | solution.py:15
  64.9 3.2 %gather_fusion = bf16[1024,64]{1,0:T(8,128)(2,1)S(1)} fusion(bf16[2048,64]{1,0:T(8,128)(2,1)S(1)} %reshape.146, s32[1024]{0:T(1024)S(1)} %broadcast_clamp_fusion), kind=kCustom, calls=%fused_computation | custom fusion | bytes 266240 | tf_op jit(solution)/shard_map/gather | solution.py:61
  68.3 0.5 broadcast.57
  68.8 1.4 reduce.6
  70.2 0.7 reshape.192
  71.0 14.7 %all-to-all-start.1 = ((bf16[32,2,1024]{2,1,0:T(2,128)(2,1)}), bf16[32,2,1024]{2,1,0:T(2,128)(2,1)S(1)}, u32[]{:S(2)}, u32[]{:S(2)}) async-start(bf16[32,2,1024]{2,1,0:T(2,128)(2,1)} %reshape.192), calls=%async_computation.1 | async-start | bytes 262144 | tf_op jit(solution)/shard_map/all_to_all | solution.py:62
  85.8 0.5 reshape.150
  86.3 1.3 fusion.28
  87.6 1.3 fusion.32
  88.9 0.3 fusion.16
  89.2 1.3 fusion.36
  90.5 12.9 %all-to-all-done.1 = bf16[32,2,1024]{2,1,0:T(2,128)(2,1)S(1)} async-done(((bf16[32,2,1024]{2,1,0:T(2,128)(2,1)}), bf16[32,2,1024]{2,1,0:T(2,128)(2,1)S(1)}, u32[]{:S(2)}, u32[]{:S(2)}) %all-to-all-start.1) | async-done | bytes 131104 | tf_op jit(solution)/shard_map/all_to_all | solution.py:62
  103.6 0.7 reduce.7
  104.3 0.7 reshape.194
  105.0 3.8 %all-to-all-start.2 = ((bf16[32,2,1024]{2,1,0:T(2,128)(2,1)}), bf16[32,2,1024]{2,1,0:T(2,128)(2,1)S(1)}, u32[]{:S(2)}, u32[]{:S(2)}) async-start(bf16[32,2,1024]{2,1,0:T(2,128)(2,1)} %reshape.194), calls=%async_computation.2 | async-start | bytes 262144 | tf_op jit(solution)/shard_map/all_to_all | solution.py:69
  108.9 0.3 fusion.15
  109.2 1.3 fusion.40
  110.4 16.1 %all-to-all-done.2 = bf16[32,2,1024]{2,1,0:T(2,128)(2,1)S(1)} async-done(((bf16[32,2,1024]{2,1,0:T(2,128)(2,1)}), bf16[32,2,1024]{2,1,0:T(2,128)(2,1)S(1)}, u32[]{:S(2)}, u32[]{:S(2)}) %all-to-all-start.2) | async-done | bytes 131104 | tf_op jit(solution)/shard_map/all_to_all | solution.py:69
  126.6 0.7 convert_reduce_fusion
  127.3 1.0 reshape.167
  128.4 7.4 %scatter_custom_fusion = f32[2048,64]{1,0:T(8,128)} fusion(s32[1024]{0:T(1024)S(1)} %bitcast.91, f32[1024,64]{1,0:T(8,128)} %reshape.167, f32[]{:T(128)} %constant.4.clone.1), kind=kCustom, calls=%fused_computation.25 | custom fusion | flops 65536 | bytes 524800 | tf_op jit(solution)/shard_map/scatter-add | solution.py:82
  135.8 3.0 %fusion.12 = bf16[8,16,16,64]{3,2,1,0:T(8,128)(2,1)S(1)} fusion(f32[8,16,16,64]{3,2,1,0:T(8,128)} %bitcast.88, f32[8,16,16,64]{3,2,1,0:T(8,128)S(1)} %fusion.16, f32[8,16,16,64]{3,2,1,0:T(8,128)S(1)} %fusion.15, f32[8,16,16,64]{3,2,1,0:T(8,128)} %fusion.28, f32[8,16,16,64]{3,2,1,0:T(8,128)} %fusion.32, f32[8,16,16,64]{3,2,1,0:T(8,128)} %fusion.36, ...), kind=kOutput, calls=%fused_computation.16 | convolution fusion | flops 17825792 | bytes 4308992 | tf_op jit(solution)/shard_map/xyze,fe->xyzf/dot_general | solution.py:30
  138.7 1.1 reshape.151
  (32 shorter events, 1.3 us)
Async XLA Ops:
  0.0 50.0 %copy-start = (bf16[64,64]{1,0:T(8,128)(2,1)S(1)}, bf16[64,64]{1,0:T(8,128)(2,1)}, u32[]{:S(2)}) copy-start(bf16[64,64]{1,0:T(8,128)(2,1)} %param.8) | copy-start | bytes 24580
  0.0 30.3 %copy-start.1 = (bf16[8,16,1024]{2,1,0:T(8,128)(2,1)S(1)}, bf16[8,16,1024]{2,1,0:T(8,128)(2,1)}, u32[]{:S(2)}) copy-start(bf16[8,16,1024]{2,1,0:T(8,128)(2,1)} %param.7) | copy-start | bytes 786436
  0.0 40.3 %all-to-all-start = ((s32[32,1,32]{2,1,0:T(1,128)}), s32[32,1,32]{2,1,0:T(1,128)S(1)}, u32[]{:S(2)}, u32[]{:S(2)}) async-start(s32[32,1,32]{2,1,0:T(1,128)} %bitcast.90), calls=%async_computation | async-start | bytes 32768 | tf_op jit(solution)/shard_map/all_to_all | solution.py:60
  19.7 10.5 %collective-permute-start = (bf16[8,1,1024]{2,1,0:T(2,128)(2,1)S(1)}, bf16[8,1,1024]{2,1,0:T(2,128)(2,1)S(1)}, u32[]{:S(2)}, u32[]{:S(2)}) collective-permute-start(bf16[8,1,1024]{2,1,0:T(2,128)(2,1)S(1)} %get-tuple-element.11), channel_id=1, source_target_pairs={{0,32},{32,64},{64,96},{96,128},{128,160},{160,192},{192,224},{224... | collective-permute-start | bytes 49160 | tf_op jit(solution)/shard_map/ppermute | solution.py:12
  22.4 7.9 %collective-permute-start.1 = (bf16[8,1,1024]{2,1,0:T(2,128)(2,1)S(1)}, bf16[8,1,1024]{2,1,0:T(2,128)(2,1)S(1)}, u32[]{:S(2)}, u32[]{:S(2)}) collective-permute-start(bf16[8,1,1024]{2,1,0:T(2,128)(2,1)S(1)} %get-tuple-element.12), channel_id=1, source_target_pairs={{32,0},{64,32},{96,64},{128,96},{160,128},{192,160},{224,192},{256... | collective-permute-start | bytes 49160 | tf_op jit(solution)/shard_map/ppermute | solution.py:15
  30.3 11.3 %collective-permute-start.2 = (bf16[1,18,1024]{2,1,0:T(8,128)(2,1)S(1)}, bf16[1,18,1024]{2,1,0:T(8,128)(2,1)S(1)}, u32[]{:S(2)}, u32[]{:S(2)}) collective-permute-start(bf16[1,18,1024]{2,1,0:T(8,128)(2,1)S(1)} %get-tuple-element.7), channel_id=1, source_target_pairs={{0,1},{1,2},{2,3},{3,4},{4,5},{5,6},{6,7},{7,8},{8,9},{9,10},{10,1... | collective-permute-start | bytes 110600 | tf_op jit(solution)/shard_map/ppermute | solution.py:12
  38.3 9.3 %collective-permute-start.3 = (bf16[1,18,1024]{2,1,0:T(8,128)(2,1)S(1)}, bf16[1,18,1024]{2,1,0:T(8,128)(2,1)S(1)}, u32[]{:S(2)}, u32[]{:S(2)}) collective-permute-start(bf16[1,18,1024]{2,1,0:T(8,128)(2,1)S(1)} %get-tuple-element.8), channel_id=1, source_target_pairs={{1,0},{2,1},{3,2},{4,3},{5,4},{6,5},{7,6},{8,7},{9,8},{10,9},{11,1... | collective-permute-start | bytes 110600 | tf_op jit(solution)/shard_map/ppermute | solution.py:15
  41.6 6.7 %copy-start.2 = (bf16[6,64,64]{2,1,0:T(8,128)(2,1)S(1)}, bf16[6,64,64]{2,1,0:T(8,128)(2,1)}, u32[]{:S(2)}) copy-start(bf16[6,64,64]{2,1,0:T(8,128)(2,1)} %param.9) | copy-start | bytes 147460
  50.9 8.1 %collective-permute-start.4 = (bf16[8,1,1024]{2,1,0:T(2,128)(2,1)S(1)}, bf16[8,1,1024]{2,1,0:T(2,128)(2,1)S(1)}, u32[]{:S(2)}, u32[]{:S(2)}) collective-permute-start(bf16[8,1,1024]{2,1,0:T(2,128)(2,1)S(1)} %get-tuple-element.9), channel_id=1, source_target_pairs={{0,32},{32,64},{64,96},{96,128},{128,160},{160,192},{192,224},{224... | collective-permute-start | bytes 49160 | tf_op jit(solution)/shard_map/ppermute | solution.py:12
  52.8 7.1 %collective-permute-start.5 = (bf16[8,1,1024]{2,1,0:T(2,128)(2,1)S(1)}, bf16[8,1,1024]{2,1,0:T(2,128)(2,1)S(1)}, u32[]{:S(2)}, u32[]{:S(2)}) collective-permute-start(bf16[8,1,1024]{2,1,0:T(2,128)(2,1)S(1)} %get-tuple-element.10), channel_id=1, source_target_pairs={{32,0},{64,32},{96,64},{128,96},{160,128},{192,160},{224,192},{256... | collective-permute-start | bytes 49160 | tf_op jit(solution)/shard_map/ppermute | solution.py:15
  59.9 25.7 %collective-permute-start.6 = (bf16[1,18,1024]{2,1,0:T(8,128)(2,1)S(1)}, bf16[1,18,1024]{2,1,0:T(8,128)(2,1)S(1)}, u32[]{:S(2)}, u32[]{:S(2)}) collective-permute-start(bf16[1,18,1024]{2,1,0:T(8,128)(2,1)S(1)} %get-tuple-element.5), channel_id=1, source_target_pairs={{0,1},{1,2},{2,3},{3,4},{4,5},{5,6},{6,7},{7,8},{8,9},{9,10},{10,1... | collective-permute-start | bytes 110600 | tf_op jit(solution)/shard_map/ppermute | solution.py:12
  63.0 22.7 %collective-permute-start.7 = (bf16[1,18,1024]{2,1,0:T(8,128)(2,1)S(1)}, bf16[1,18,1024]{2,1,0:T(8,128)(2,1)S(1)}, u32[]{:S(2)}, u32[]{:S(2)}) collective-permute-start(bf16[1,18,1024]{2,1,0:T(8,128)(2,1)S(1)} %get-tuple-element.6), channel_id=1, source_target_pairs={{1,0},{2,1},{3,2},{4,3},{5,4},{6,5},{7,6},{8,7},{9,8},{10,9},{11,1... | collective-permute-start | bytes 110600 | tf_op jit(solution)/shard_map/ppermute | solution.py:15
  71.0 32.4 %all-to-all-start.1 = ((bf16[32,2,1024]{2,1,0:T(2,128)(2,1)}), bf16[32,2,1024]{2,1,0:T(2,128)(2,1)S(1)}, u32[]{:S(2)}, u32[]{:S(2)}) async-start(bf16[32,2,1024]{2,1,0:T(2,128)(2,1)} %reshape.192), calls=%async_computation.1 | async-start | bytes 262144 | tf_op jit(solution)/shard_map/all_to_all | solution.py:62
  89.2 14.3 %copy-start.3 = (bf16[1,1,32,2048]{3,2,1,0:T(8,128)(2,1)S(1)}, bf16[1,1,32,2048]{3,2,1,0:T(8,128)(2,1)}, u32[]{:S(2)}) copy-start(bf16[1,1,32,2048]{3,2,1,0:T(8,128)(2,1)} %param.12) | copy-start | bytes 393220
  89.2 14.3 %copy-start.4 = (bf16[1,1,32,2048]{3,2,1,0:T(8,128)(2,1)S(1)}, bf16[1,1,32,2048]{3,2,1,0:T(8,128)(2,1)}, u32[]{:S(2)}) copy-start(bf16[1,1,32,2048]{3,2,1,0:T(8,128)(2,1)} %param.13) | copy-start | bytes 393220
  105.0 21.5 %all-to-all-start.2 = ((bf16[32,2,1024]{2,1,0:T(2,128)(2,1)}), bf16[32,2,1024]{2,1,0:T(2,128)(2,1)S(1)}, u32[]{:S(2)}, u32[]{:S(2)}) async-start(bf16[32,2,1024]{2,1,0:T(2,128)(2,1)} %reshape.194), calls=%async_computation.2 | async-start | bytes 262144 | tf_op jit(solution)/shard_map/all_to_all | solution.py:69
where the time goes:
time: 140 us
  starting transfers between devices  68.1 us (49%)
  waiting for transfers between devices  35.9 us (26%)
  local copies, waits for them, and re-layouts  12.5 us (9%)
  other arithmetic  12.1 us (9%)
  matrix products  10.8 us (8%)
    all_to_all x1, starting transfers between devices, on_device(): lax.all_to_all(own_index, 'gx', split_axis=0, concat_axis=0, tiled=True)  18.7 us
    all_to_all x1, waiting for transfers between devices, on_device(): lax.all_to_all(misfit.reshape(tiles, slots * elems).astype(jnp.bfloat16),...  16.1 us
    ppermute x4, starting transfers between devices, with_halo(): lax.ppermute(lax.slice_in_dim(block, block.shape[dim] - width, None, axis...  15.6 us
    ppermute x4, starting transfers between devices, with_halo(): lax.ppermute(lax.slice_in_dim(block, 0, width, axis=dim), axis, backward)  15.2 us
    all_to_all x1, starting transfers between devices, on_device(): lax.all_to_all(fetched, 'gx', split_axis=0, concat_axis=0, tiled=True)  14.7 us
    all_to_all x1, waiting for transfers between devices, on_device(): lax.all_to_all(fetched, 'gx', split_axis=0, concat_axis=0, tiled=True)  12.9 us
    scatter-add x1, other arithmetic, on_device(): data = jnp.zeros((rows_x * rows_y * thick, elems), jnp.float32).at[got_in...  7.39 us
    dot_general x12, matrix products, spread(): jnp.einsum(form, nearby[which], couple[which], preferred_element_type=jnp...  7.37 us
  transfers between devices with their start and end apart: 11, of which 4 were waited for; matrix products, arithmetic and copies ran while one was open for 12% of the time, Pallas kernels for 0%

commit v1 on v0

v1 whole, which is shorter than its diff:
```python
import functools

import jax
import jax.numpy as jnp
from jax import lax
from jax.experimental import pallas as pl
from jax.experimental.pallas import tpu as pltpu
from jax.sharding import PartitionSpec as P

BF = jnp.bfloat16
F32 = jnp.float32
MESH = pl.DeviceIdType.MESH
GROUP = 8


def dot(a, b):
    return jnp.dot(a, b, preferred_element_type=F32)


def dot_t(a, b):
    return lax.dot_general(a, b, (((1,), (1,)), ((), ())), preferred_element_type=F32)


def iota(shape, dim):
    return lax.broadcasted_iota(jnp.int32, shape, dim)


def put_wide(grid, row, values):
    for j in range(8):
        grid[j, row:row + values.shape[0], :] = values[:, j * 128:j * 128 + 128]


def put_column(grid, row, values):
    for j in range(8):
        grid[j, pl.ds(row, 8, stride=32), :] = values[:, j * 128:j * 128 + 128]


def get_column(grid, row):
    return jnp.concatenate([grid[j, pl.ds(row, 8, stride=32), :] for j in range(8)], axis=1)


def shifted(grid, jb, row, start, stop):
    return jnp.concatenate(
        [
            jnp.concatenate(
                [grid[2 * jb + k, x * 32 + row:x * 32 + row + 16, :] for x in range(start, stop)],
                axis=0,
            )
            for k in range(2)
        ],
        axis=1,
    )


def kernel(
    n, m,
    field, center, couple, index, counts, assays, weights,
    out,
    u, av, wv, iv, cv, kc, kd,
    stage, msg, got, code, gotcode,
    ysend, yrecv, csend, crecv,
    uf, uc, edge, imf, imx, wst, prior, rhs, acc, res,
    in_sem, out_sem, halo_send, halo_recv, list_send, list_recv, code_send, code_recv,
):
    gy, gx = lax.axis_index("gy"), lax.axis_index("gx")
    left, right = lax.rem(gx + n - 1, n), lax.rem(gx + 1, n)
    down, up = lax.rem(gy + m - 1, m), lax.rem(gy + 1, m)

    ins = [
        pltpu.make_async_copy(assays, av, in_sem.at[0]),
        pltpu.make_async_copy(weights, wv, in_sem.at[1]),
        pltpu.make_async_copy(field, u.at[pl.ds(2, 8)], in_sem.at[2]),
        pltpu.make_async_copy(index, iv, in_sem.at[3]),
        pltpu.make_async_copy(counts, cv, in_sem.at[4]),
        pltpu.make_async_copy(center, kc, in_sem.at[5]),
        pltpu.make_async_copy(couple, kd, in_sem.at[6]),
    ]
    for one in ins:
        one.start()

    barrier = pltpu.get_barrier_semaphore()

    def greet(d, _):
        pl.semaphore_signal(
            barrier, inc=1, device_id=(gy, lax.rem(gx + d, n)), device_id_type=MESH
        )
        return 0

    lax.fori_loop(1, n, greet, 0)
    for who in ((down, gx), (up, gx), (down, left), (down, right), (up, left), (up, right)):
        pl.semaphore_signal(barrier, inc=1, device_id=who, device_id_type=MESH)

    for which, (copy, src) in enumerate(((ins[0], av), (ins[1], wv))):
        copy.wait()
        for j in range(16):
            stage[pl.ds(j, n, stride=16), :] = src[:, j * 128:(j + 1) * 128].astype(F32)
        msg[:, which * 16:(which + 1) * 16, :] = stage[...].reshape(n, 16, 128).astype(BF)

    ins[3].wait()
    ins[4].wait()
    row, lane = iota((n, n), 0), iota((n, n), 1)
    count = jnp.sum(jnp.where(row == lane, cv[...].astype(F32), 0.0), axis=1, keepdims=True)
    used = iota((n, 32), 1).astype(F32) < count
    cells = jnp.where(used, iv[...], -1)
    pick_s, pick_l = iota((32, 128), 0), iota((32, 128), 1)
    pick = jnp.where(
        pick_s == 2 * lax.rem(pick_l, 16) + lax.rem(pick_l, 32) // 16, 1.0, 0.0
    ).astype(BF)
    high = dot(jnp.right_shift(cells, 4).astype(F32).astype(BF), pick)
    low = dot(jnp.bitwise_and(cells, 15).astype(F32).astype(BF), pick)
    codes = (high * 16.0 + low).astype(jnp.int32)
    for t in range(n):
        code[t] = codes[t:t + 1]

    ins[2].wait()
    for x in range(8):
        put_wide(uf, (x + 1) * 32 + 8, u[x + 2].astype(F32))

    def rows_at(y):
        return get_column(uf, 40 + y)

    ysend[0] = jnp.concatenate([rows_at(0), rows_at(1)], axis=0).astype(BF)
    ysend[1] = jnp.concatenate([rows_at(15), rows_at(14)], axis=0).astype(BF)
    for c, (x, y) in enumerate(((7, 15), (7, 0), (0, 15), (0, 0))):
        place = (x + 1) * 32 + 8 + y
        for j in range(8):
            csend[c, j:j + 1, :] = uf[j, place:place + 1, :]

    pl.semaphore_wait(barrier, n - 1 + 6)

    def remote(src, dst, send, recv, who):
        return pltpu.make_async_remote_copy(
            src_ref=src, dst_ref=dst, send_sem=send, recv_sem=recv,
            device_id=who, device_id_type=MESH,
        )

    halos = [
        remote(u.at[pl.ds(2, 2)], u.at[pl.ds(10, 2)], halo_send.at[0], halo_recv.at[0], (gy, left)),
        remote(u.at[pl.ds(8, 2)], u.at[pl.ds(0, 2)], halo_send.at[1], halo_recv.at[1], (gy, right)),
        remote(ysend.at[0], yrecv.at[1], halo_send.at[2], halo_recv.at[2], (down, gx)),
        remote(ysend.at[1], yrecv.at[0], halo_send.at[3], halo_recv.at[3], (up, gx)),
        remote(csend.at[0], crecv.at[0], halo_send.at[4], halo_recv.at[4], (up, right)),
        remote(csend.at[1], crecv.at[1], halo_send.at[5], halo_recv.at[5], (down, right)),
        remote(csend.at[2], crecv.at[2], halo_send.at[6], halo_recv.at[6], (up, left)),
        remote(csend.at[3], crecv.at[3], halo_send.at[7], halo_recv.at[7], (down, left)),
    ]
    for one in halos:
        one.start()

    def send_code(d, _):
        to = lax.rem(gx + d, n)
        remote(code.at[to], gotcode.at[d - 1], code_send.at[0], code_recv.at[0], (gy, to)).start()
        return 0

    lax.fori_loop(1, n, send_code, 0)

    def send_list(d, _):
        to = lax.rem(gx + d, n)
        remote(
            msg.at[to], got.at[d - 1], list_send.at[0], list_recv.at[(d - 1) // GROUP], (gy, to)
        ).start()
        return 0

    lax.fori_loop(1, n, send_list, 0)
    got[n - 1] = msg[gx]
    gotcode[n - 1] = code[gx]

    ins[5].wait()
    ins[6].wait()
    spread = jnp.where(lax.rem(iota((256, 64), 0), 64) == iota((256, 64), 1), 1.0, 0.0).astype(BF)
    rb, cb = iota((256, 256), 0) // 64, iota((256, 256), 1) // 64

    def tiled(block, flip):
        tall = (dot_t if flip else dot)(spread, block).astype(BF)
        return dot_t(tall, spread)

    for s in range(2):
        mid = tiled(kc[...], s == 1)
        above = tiled(kd[5 if s else 4], s == 1)
        below = tiled(kd[4 if s else 5], s == 1)
        for half in range(2):
            zr = rb - 2 + 4 * half
            window = jnp.where(zr == cb, mid, 0.0)
            window = jnp.where(zr == cb + 1, -above, window)
            window = jnp.where(zr == cb - 1, -below, window)
            wst[s, half * 256:half * 256 + 256, :] = window.astype(BF)
        for d in range(4):
            wst[s, 512 + d * 256:768 + d * 256, :] = jnp.where(
                rb == cb, -tiled(kd[d], s == 1), 0.0
            ).astype(BF)

    has_left, has_right, has_down, has_up = gx > 0, gx < n - 1, gy > 0, gy < m - 1
    for one in halos:
        one.wait_recv()
    zero = jnp.zeros((), F32)
    for slot, ok in ((0, has_left), (10, has_right)):
        for x in (slot, slot + 1):
            u[x] = jnp.where(ok, u[x].astype(F32), zero).astype(BF)
    put_wide(uf, 8, u[1].astype(F32))
    put_wide(uf, 9 * 32 + 8, u[10].astype(F32))
    low_y = jnp.where(has_down, yrecv[0].astype(F32), zero)
    high_y = jnp.where(has_up, yrecv[1].astype(F32), zero)
    put_column(uf, 32 + 7, low_y[0:8])
    put_column(uf, 32 + 24, high_y[0:8])
    for c, (x, y, ok) in enumerate(
        ((-1, -1, has_left & has_down), (-1, 16, has_left & has_up),
         (8, -1, has_right & has_down), (8, 16, has_right & has_up))
    ):
        place = (x + 1) * 32 + 8 + y
        for j in range(8):
            uf[j, place:place + 1, :] = jnp.where(ok, crecv[c, j:j + 1, :], zero)
    uc[:, 0:128] = jnp.zeros((160, 128), BF)
    uc[:, 1152:1280] = jnp.zeros((160, 128), BF)
    imx[:, 0:128] = jnp.zeros((160, 128), BF)
    imx[:, 1152:1280] = jnp.zeros((160, 128), BF)
    edge[:, :, 0:128] = jnp.zeros((5, 16, 128), BF)
    edge[:, :, 1152:1280] = jnp.zeros((5, 16, 128), BF)
    for x in range(10):
        uc[x * 16:x * 16 + 16, 128:1152] = u[x + 1]

    def pair(first, second):
        return jnp.concatenate([first, second], axis=0).astype(BF)

    edge[0, :, 128:1152] = pair(low_y[0:8], high_y[0:8])
    edge[1, :, 128:1152] = pair(get_column(uf, 64 + 7), get_column(uf, 64 + 24))
    edge[2, :, 128:1152] = pair(get_column(uf, 7), get_column(uf, 24))
    edge[3, :, 128:1152] = pair(rows_at(0), high_y[8:16])
    edge[4, :, 128:1152] = pair(low_y[8:16], rows_at(15))

    left_ok = jnp.where(has_left, 1.0, 0.0)
    right_ok = jnp.where(has_right, 1.0, 0.0)
    down_ok = jnp.where(has_down, 1.0, 0.0)
    up_ok = jnp.where(has_up, 1.0, 0.0)

    def image_part(jb, _):
        here = pl.ds(pl.multiple_of(jb * 256, 128), 256)
        inner = pl.ds(pl.multiple_of(jb * 256 + 128, 128), 256)
        window = pl.ds(pl.multiple_of(jb * 256, 128), 512)
        total = dot(uc[:, window], wst[0, 0:512])
        total += dot(u[2:12, :, here].reshape(160, 256), wst[0, 512:768])
        total += dot(u[0:10, :, here].reshape(160, 256), wst[0, 768:1024])
        plus = shifted(uf, jb, 9, 0, 10)
        total += dot(plus.astype(BF), wst[0, 1024:1280])
        minus = shifted(uf, jb, 7, 0, 10)
        total += dot(minus.astype(BF), wst[0, 1280:1536])
        rounded = total.astype(BF).astype(F32)
        for x in range(10):
            part = rounded[x * 16:x * 16 + 16]
            if x == 0:
                part = part * left_ok
            if x == 9:
                part = part * right_ok
            imx[x * 16:x * 16 + 16, inner] = part.astype(BF)
            for k in range(2):
                imf[2 * jb + k, x * 32 + 8:x * 32 + 24, :] = part[:, k * 128:k * 128 + 128]
        rim = dot(edge[0, :, window], wst[0, 0:512])
        for d in range(4):
            rim += dot(edge[d + 1, :, inner], wst[0, 512 + d * 256:768 + d * 256])
        rim = rim.astype(BF).astype(F32)
        for k in range(2):
            lanes = slice(k * 128, k * 128 + 128)
            imf[2 * jb + k, pl.ds(39, 8, stride=32), :] = rim[0:8, lanes] * down_ok
            imf[2 * jb + k, pl.ds(56, 8, stride=32), :] = rim[8:16, lanes] * up_ok
        return 0

    lax.fori_loop(0, 4, image_part, 0)

    def prior_part(jb, _):
        here = pl.ds(pl.multiple_of(jb * 256, 128), 256)
        inner = pl.ds(pl.multiple_of(jb * 256 + 128, 128), 256)
        window = pl.ds(pl.multiple_of(jb * 256, 128), 512)
        total = dot(imx[16:144, window], wst[1, 0:512])
        total += dot(imx[0:128, inner], wst[1, 512:768])
        total += dot(imx[32:160, inner], wst[1, 768:1024])
        minus = shifted(imf, jb, 7, 1, 9)
        total += dot(minus.astype(BF), wst[1, 1024:1280])
        plus = shifted(imf, jb, 9, 1, 9)
        total += dot(plus.astype(BF), wst[1, 1280:1536])
        prior[:, here] = total
        return 0

    lax.fori_loop(0, 4, prior_part, 0)

    some = gotcode.at[pl.ds(0, n - 1)]
    remote(some, some, code_send.at[0], code_recv.at[0], (gy, right)).wait_recv()
    low_lane = iota((GROUP * 16, 128), 1) < 64
    cell16 = iota((128, GROUP * 32), 0) * 16
    quarter = iota((1, 128), 1) // 32
    groups = n // GROUP
    for g in range(groups):
        first = g * GROUP
        arriving = GROUP if g < groups - 1 else GROUP - 1
        part = got.at[pl.ds(first, arriving)]
        remote(part, part, list_send.at[0], list_recv.at[g], (gy, right)).wait_recv()
        a = got[first:first + GROUP, 0:16, :].astype(F32).reshape(GROUP * 16, 128)
        w = got[first:first + GROUP, 16:32, :].astype(F32).reshape(GROUP * 16, 128)
        p = a * w
        hi = p.astype(BF).astype(F32)
        lo = p - hi
        wr, hir, lor = (pltpu.roll(v, 64, 1) for v in (w, hi, lo))
        for parity, slots, one, two in (
            (0, 0, jnp.where(low_lane, hi, wr), lo),
            (0, 1, jnp.where(low_lane, hir, w), lor),
            (1, 0, jnp.where(low_lane, w, hir), lor),
            (1, 1, jnp.where(low_lane, wr, hi), lo),
        ):
            at = slice(slots * 16, slots * 16 + 16)
            rhs[parity, :, at, 0:128] = one.astype(BF).reshape(GROUP, 16, 128)
            rhs[parity, :, at, 128:256] = two.astype(BF).reshape(GROUP, 16, 128)
        keys = []
        for q in range(GROUP // 4):
            key = gotcode[first + 4 * q]
            for o in range(1, 4):
                key = jnp.where(quarter == o, gotcode[first + 4 * q + o], key)
            keys.append(key)
        key = jnp.concatenate(keys, axis=1)

        def layer(zz, _, g=g, key=key):
            for parity in range(2):
                z = 2 * zz + parity
                hit = jnp.where(cell16 == key - z, 1.0, 0.0).astype(BF)
                part = dot(hit, rhs[parity].reshape(GROUP * 32, 256))
                acc[z] = part if g == 0 else acc[z] + part
            return 0

        lax.fori_loop(0, 8, layer, 0)

    low_out = iota((128, 128), 1) < 64
    for zz in range(8):
        even, odd = acc[2 * zz], acc[2 * zz + 1]
        lanes = slice(zz * 128, zz * 128 + 128)
        s1 = jnp.where(low_out, even[:, 0:128] + even[:, 128:256], odd[:, 0:128] + odd[:, 128:256])
        s0 = pltpu.roll(jnp.where(low_out, odd[:, 0:128], even[:, 0:128]), 64, 1)
        own = u[2:10, :, lanes].astype(F32).reshape(128, 128)
        grad = s1 - own * s0 - prior[:, lanes]
        res[:, :, lanes] = grad.astype(BF).reshape(8, 16, 128)

    put = pltpu.make_async_copy(res, out, out_sem.at[0])
    put.start()
    for one in halos:
        one.wait_send()
    remote(some, some, code_send.at[0], code_recv.at[0], (gy, right)).wait_send()
    every = got.at[pl.ds(0, n - 1)]
    remote(every, every, list_send.at[0], list_recv.at[0], (gy, right)).wait_send()
    put.wait()


def on_device(field, center_block, couple_blocks, cell_index, slot_counts, assays, assay_weights):
    n, m = lax.axis_size("gx"), lax.axis_size("gy")
    vm, dma = pltpu.VMEM, pltpu.SemaphoreType.DMA
    i32 = jnp.int32
    return pl.pallas_call(
        functools.partial(kernel, n, m),
        out_shape=jax.ShapeDtypeStruct(field.shape, BF),
        in_specs=[pl.BlockSpec(memory_space=pl.ANY)] * 7,
        out_specs=pl.BlockSpec(memory_space=pl.ANY),
        scratch_shapes=[
            vm((12, 16, 1024), BF),
            vm((n, 2048), BF),
            vm((n, 2048), BF),
            vm((n, 32), i32),
            vm((1, n), i32),
            vm((64, 64), BF),
            vm((6, 64, 64), BF),
            vm((n * 16, 128), F32),
            vm((n, 32, 128), BF),
            vm((n, 32, 128), BF),
            vm((n, 1, 128), i32),
            vm((n, 1, 128), i32),
            vm((2, 16, 1024), BF),
            vm((2, 16, 1024), BF),
            vm((4, 8, 128), F32),
            vm((4, 8, 128), F32),
            vm((8, 320, 128), F32),
            vm((160, 1280), BF),
            vm((5, 16, 1280), BF),
            vm((8, 320, 128), F32),
            vm((160, 1280), BF),
            vm((2, 1536, 256), BF),
            vm((128, 1024), F32),
            vm((2, GROUP, 32, 256), BF),
            vm((16, 128, 256), F32),
            vm((8, 16, 1024), BF),
            dma((7,)), dma((1,)), dma((8,)), dma((8,)),
            dma((1,)), dma((n // GROUP,)), dma((1,)), dma((1,)),
        ],
        compiler_params=pltpu.CompilerParams(
            collective_id=0, has_side_effects=True, vmem_limit_bytes=40 * 1024 * 1024
        ),
    )(
        field, center_block, couple_blocks, cell_index.reshape(n, 32),
        slot_counts.reshape(1, n), assays.reshape(n, 2048), assay_weights.reshape(n, 2048),
    )


def solution(mesh):
    in_specs = (
        P("gx", "gy", None),
        P(),
        P(),
        P("gy", "gx", None, None),
        P("gy", "gx", None),
        P("gy", "gx", None, None),
        P("gy", "gx", None, None),
    )
    return jax.shard_map(
        on_device, mesh=mesh, in_specs=in_specs, out_specs=P("gx", "gy", None), check_vma=False
    )
```

time: 140 us -> 51.7 us (0.37)
  the two profiles are of different devices: /device:TPU:3 before, /device:TPU:1 now
where the time goes in v1:
time: 51.7 us; the launch traced here: 51.3 us
  Pallas kernels  44.9 us (87%)
  local copies, waits for them, and re-layouts  6.44 us (12%)
    pallas_call x1, Pallas kernels, on_device(): pl.pallas_call(functools.partial(kernel, n, m), out_shape=jax.ShapeDtypeS...  44.9 us
    unnamed x15, local copies, waits for them, and re-layouts  6.44 us

profile of v1, /device:TPU:1, one launch (start us, length us, event | category | flops | bytes accessed | tf_op | source)
XLA Modules:
  0.0 51.3 jit_solution(4689752209243914721)
XLA Ops:
  0.0 0.0 copy-start.6
  0.0 0.7 %copy-done.6 = s32[1,1,32]{2,1,0:T(1,128)S(1)} copy-done((s32[1,1,32]{2,1,0:T(1,128)S(1)}, s32[1,1,32]{2,1,0:T(1,128)}, u32[]{:S(2)}) %copy-start.6) | copy-done | bytes 152
  0.7 0.0 copy-start
  0.7 0.9 %copy-done = bf16[8,16,1024]{2,1,0:T(8,128)(2,1)S(1)} copy-done((bf16[8,16,1024]{2,1,0:T(8,128)(2,1)S(1)}, bf16[8,16,1024]{2,1,0:T(8,128)(2,1)}, u32[]{:S(2)}) %copy-start) | copy-done | bytes 262168
  1.6 0.0 copy-start.1
  1.6 0.9 %copy-done.1 = bf16[1,1,32,2048]{3,2,1,0:T(8,128)(2,1)S(1)} copy-done((bf16[1,1,32,2048]{3,2,1,0:T(8,128)(2,1)S(1)}, bf16[1,1,32,2048]{3,2,1,0:T(8,128)(2,1)}, u32[]{:S(2)}) %copy-start.1) | copy-done | bytes 131096
  2.5 0.0 copy-start.2
  2.5 0.9 %copy-done.2 = bf16[1,1,32,2048]{3,2,1,0:T(8,128)(2,1)S(1)} copy-done((bf16[1,1,32,2048]{3,2,1,0:T(8,128)(2,1)S(1)}, bf16[1,1,32,2048]{3,2,1,0:T(8,128)(2,1)}, u32[]{:S(2)}) %copy-start.2) | copy-done | bytes 131096
  3.4 0.0 copy-start.3
  3.4 0.9 %copy-done.3 = bf16[6,64,64]{2,1,0:T(8,128)(2,1)S(1)} copy-done((bf16[6,64,64]{2,1,0:T(8,128)(2,1)S(1)}, bf16[6,64,64]{2,1,0:T(8,128)(2,1)}, u32[]{:S(2)}) %copy-start.3) | copy-done | bytes 49176
  4.3 0.0 copy-start.4
  4.3 0.7 %copy-done.4 = bf16[64,64]{1,0:T(8,128)(2,1)S(1)} copy-done((bf16[64,64]{1,0:T(8,128)(2,1)S(1)}, bf16[64,64]{1,0:T(8,128)(2,1)}, u32[]{:S(2)}) %copy-start.4) | copy-done | bytes 8216
  5.0 0.0 copy-start.5
  5.0 0.7 %copy-done.5 = s32[1,1,32,32]{3,2,1,0:T(8,128)S(1)} copy-done((s32[1,1,32,32]{3,2,1,0:T(8,128)S(1)}, s32[1,1,32,32]{3,2,1,0:T(8,128)}, u32[]{:S(2)}) %copy-start.5) | copy-done | bytes 4120
  5.7 44.9 %shard_map.73 = bf16[8,16,1024]{2,1,0:T(8,128)(2,1)S(1)} custom-call(bf16[8,16,1024]{2,1,0:T(8,128)(2,1)S(1)} %copy-done, bf16[64,64]{1,0:T(8,128)(2,1)S(1)} %copy-done.4, bf16[6,64,64]{2,1,0:T(8,128)(2,1)S(1)} %copy-done.3, s32[32,32]{1,0:T(8,128)S(1)} %bitcast.6, s32[1,32]{1,0:T(1,128)S(1)} %bitcast.7, bf16[32,2048]{1,0:T(8,128)(2,1)S(1)} %bitcast.4, ...), custom_call_target="tpu_custom_call" | custom-call | tf_op jit(solution)/shard_map/pallas_call | solution.py:352
  50.6 0.7 %copy.9 = bf16[8,16,1024]{2,1,0:T(8,128)(2,1)} copy(bf16[8,16,1024]{2,1,0:T(8,128)(2,1)S(1)} %shard_map.73) | data formatting | bytes 524288
Async XLA Ops:
  0.0 0.7 %copy-start.6 = (s32[1,1,32]{2,1,0:T(1,128)S(1)}, s32[1,1,32]{2,1,0:T(1,128)}, u32[]{:S(2)}) copy-start(s32[1,1,32]{2,1,0:T(1,128)} %param.11) | copy-start | bytes 388
  0.7 0.9 %copy-start = (bf16[8,16,1024]{2,1,0:T(8,128)(2,1)S(1)}, bf16[8,16,1024]{2,1,0:T(8,128)(2,1)}, u32[]{:S(2)}) copy-start(bf16[8,16,1024]{2,1,0:T(8,128)(2,1)} %field.1) | copy-start | bytes 786436
  1.6 0.9 %copy-start.1 = (bf16[1,1,32,2048]{3,2,1,0:T(8,128)(2,1)S(1)}, bf16[1,1,32,2048]{3,2,1,0:T(8,128)(2,1)}, u32[]{:S(2)}) copy-start(bf16[1,1,32,2048]{3,2,1,0:T(8,128)(2,1)} %param.12) | copy-start | bytes 393220
  2.5 0.9 %copy-start.2 = (bf16[1,1,32,2048]{3,2,1,0:T(8,128)(2,1)S(1)}, bf16[1,1,32,2048]{3,2,1,0:T(8,128)(2,1)}, u32[]{:S(2)}) copy-start(bf16[1,1,32,2048]{3,2,1,0:T(8,128)(2,1)} %param.13) | copy-start | bytes 393220
  3.4 0.9 %copy-start.3 = (bf16[6,64,64]{2,1,0:T(8,128)(2,1)S(1)}, bf16[6,64,64]{2,1,0:T(8,128)(2,1)}, u32[]{:S(2)}) copy-start(bf16[6,64,64]{2,1,0:T(8,128)(2,1)} %couple.1) | copy-start | bytes 147460
  4.3 0.7 %copy-start.4 = (bf16[64,64]{1,0:T(8,128)(2,1)S(1)}, bf16[64,64]{1,0:T(8,128)(2,1)}, u32[]{:S(2)}) copy-start(bf16[64,64]{1,0:T(8,128)(2,1)} %center.1) | copy-start | bytes 24580
  5.0 0.7 %copy-start.5 = (s32[1,1,32,32]{3,2,1,0:T(8,128)S(1)}, s32[1,1,32,32]{3,2,1,0:T(8,128)}, u32[]{:S(2)}) copy-start(s32[1,1,32,32]{3,2,1,0:T(8,128)} %param.10) | copy-start | bytes 12292

commit v2 on v1

--- a/solution.py
+++ b/solution.py
@@ -59,7 +59,7 @@
     u, av, wv, iv, cv, kc, kd,
     stage, msg, got, code, gotcode,
     ysend, yrecv, csend, crecv,
-    uf, uc, edge, imf, imx, wst, prior, rhs, acc, res,
+    uf, uc, edge, imf, imx, wst, prior, rhs, hot, acc, res,
     in_sem, out_sem, halo_send, halo_recv, list_send, list_recv, code_send, code_recv,
 ):
     gy, gx = lax.axis_index("gy"), lax.axis_index("gx")
@@ -165,129 +165,147 @@
     got[n - 1] = msg[gx]
     gotcode[n - 1] = code[gx]
 
-    ins[5].wait()
-    ins[6].wait()
-    spread = jnp.where(lax.rem(iota((256, 64), 0), 64) == iota((256, 64), 1), 1.0, 0.0).astype(BF)
-    rb, cb = iota((256, 256), 0) // 64, iota((256, 256), 1) // 64
-
-    def tiled(block, flip):
-        tall = (dot_t if flip else dot)(spread, block).astype(BF)
-        return dot_t(tall, spread)
-
-    for s in range(2):
-        mid = tiled(kc[...], s == 1)
-        above = tiled(kd[5 if s else 4], s == 1)
-        below = tiled(kd[4 if s else 5], s == 1)
-        for half in range(2):
-            zr = rb - 2 + 4 * half
-            window = jnp.where(zr == cb, mid, 0.0)
-            window = jnp.where(zr == cb + 1, -above, window)
-            window = jnp.where(zr == cb - 1, -below, window)
-            wst[s, half * 256:half * 256 + 256, :] = window.astype(BF)
-        for d in range(4):
-            wst[s, 512 + d * 256:768 + d * 256, :] = jnp.where(
-                rb == cb, -tiled(kd[d], s == 1), 0.0
-            ).astype(BF)
-
-    has_left, has_right, has_down, has_up = gx > 0, gx < n - 1, gy > 0, gy < m - 1
-    for one in halos:
-        one.wait_recv()
-    zero = jnp.zeros((), F32)
-    for slot, ok in ((0, has_left), (10, has_right)):
-        for x in (slot, slot + 1):
-            u[x] = jnp.where(ok, u[x].astype(F32), zero).astype(BF)
-    put_wide(uf, 8, u[1].astype(F32))
-    put_wide(uf, 9 * 32 + 8, u[10].astype(F32))
-    low_y = jnp.where(has_down, yrecv[0].astype(F32), zero)
-    high_y = jnp.where(has_up, yrecv[1].astype(F32), zero)
-    put_column(uf, 32 + 7, low_y[0:8])
-    put_column(uf, 32 + 24, high_y[0:8])
-    for c, (x, y, ok) in enumerate(
-        ((-1, -1, has_left & has_down), (-1, 16, has_left & has_up),
-         (8, -1, has_right & has_down), (8, 16, has_right & has_up))
-    ):
-        place = (x + 1) * 32 + 8 + y
-        for j in range(8):
-            uf[j, place:place + 1, :] = jnp.where(ok, crecv[c, j:j + 1, :], zero)
-    uc[:, 0:128] = jnp.zeros((160, 128), BF)
-    uc[:, 1152:1280] = jnp.zeros((160, 128), BF)
-    imx[:, 0:128] = jnp.zeros((160, 128), BF)
-    imx[:, 1152:1280] = jnp.zeros((160, 128), BF)
-    edge[:, :, 0:128] = jnp.zeros((5, 16, 128), BF)
-    edge[:, :, 1152:1280] = jnp.zeros((5, 16, 128), BF)
-    for x in range(10):
-        uc[x * 16:x * 16 + 16, 128:1152] = u[x + 1]
-
-    def pair(first, second):
-        return jnp.concatenate([first, second], axis=0).astype(BF)
-
-    edge[0, :, 128:1152] = pair(low_y[0:8], high_y[0:8])
-    edge[1, :, 128:1152] = pair(get_column(uf, 64 + 7), get_column(uf, 64 + 24))
-    edge[2, :, 128:1152] = pair(get_column(uf, 7), get_column(uf, 24))
-    edge[3, :, 128:1152] = pair(rows_at(0), high_y[8:16])
-    edge[4, :, 128:1152] = pair(low_y[8:16], rows_at(15))
-
-    left_ok = jnp.where(has_left, 1.0, 0.0)
-    right_ok = jnp.where(has_right, 1.0, 0.0)
-    down_ok = jnp.where(has_down, 1.0, 0.0)
-    up_ok = jnp.where(has_up, 1.0, 0.0)
-
-    def image_part(jb, _):
-        here = pl.ds(pl.multiple_of(jb * 256, 128), 256)
-        inner = pl.ds(pl.multiple_of(jb * 256 + 128, 128), 256)
-        window = pl.ds(pl.multiple_of(jb * 256, 128), 512)
-        total = dot(uc[:, window], wst[0, 0:512])
-        total += dot(u[2:12, :, here].reshape(160, 256), wst[0, 512:768])
-        total += dot(u[0:10, :, here].reshape(160, 256), wst[0, 768:1024])
-        plus = shifted(uf, jb, 9, 0, 10)
-        total += dot(plus.astype(BF), wst[0, 1024:1280])
-        minus = shifted(uf, jb, 7, 0, 10)
-        total += dot(minus.astype(BF), wst[0, 1280:1536])
-        rounded = total.astype(BF).astype(F32)
+    def matrices():
+        ins[5].wait()
+        ins[6].wait()
+        spread = jnp.where(lax.rem(iota((256, 64), 0), 64) == iota((256, 64), 1), 1.0, 0.0).astype(BF)
+        rb, cb = iota((256, 256), 0) // 64, iota((256, 256), 1) // 64
+
+        def tiled(block, flip):
+            tall = (dot_t if flip else dot)(spread, block).astype(BF)
+            return dot_t(tall, spread)
+
+        for s in range(2):
+            mid = tiled(kc[...], s == 1)
+            above = tiled(kd[5 if s else 4], s == 1)
+            below = tiled(kd[4 if s else 5], s == 1)
+            for half in range(2):
+                zr = rb - 2 + 4 * half
+                window = jnp.where(zr == cb, mid, 0.0)
+                window = jnp.where(zr == cb + 1, -above, window)
+                window = jnp.where(zr == cb - 1, -below, window)
+                wst[s, half * 256:half * 256 + 256, :] = window.astype(BF)
+            for d in range(4):
+                wst[s, 512 + d * 256:768 + d * 256, :] = jnp.where(
+                    rb == cb, -tiled(kd[d], s == 1), 0.0
+                ).astype(BF)
+
+    def beyond():
+        has_left, has_right, has_down, has_up = gx > 0, gx < n - 1, gy > 0, gy < m - 1
+        for one in halos:
+            one.wait_recv()
+        zero = jnp.zeros((), F32)
+        for slot, ok in ((0, has_left), (10, has_right)):
+            for x in (slot, slot + 1):
+                u[x] = jnp.where(ok, u[x].astype(F32), zero).astype(BF)
+        put_wide(uf, 8, u[1].astype(F32))
+        put_wide(uf, 9 * 32 + 8, u[10].astype(F32))
+        low_y = jnp.where(has_down, yrecv[0].astype(F32), zero)
+        high_y = jnp.where(has_up, yrecv[1].astype(F32), zero)
+        put_column(uf, 32 + 7, low_y[0:8])
+        put_column(uf, 32 + 24, high_y[0:8])
+        for c, (x, y, ok) in enumerate(
+            ((-1, -1, has_left & has_down), (-1, 16, has_left & has_up),
+             (8, -1, has_right & has_down), (8, 16, has_right & has_up))
+        ):
+            place = (x + 1) * 32 + 8 + y
+            for j in range(8):
+                uf[j, place:place + 1, :] = jnp.where(ok, crecv[c, j:j + 1, :], zero)
+        uc[:, 0:128] = jnp.zeros((160, 128), BF)
+        uc[:, 1152:1280] = jnp.zeros((160, 128), BF)
+        imx[:, 0:128] = jnp.zeros((160, 128), BF)
+        imx[:, 1152:1280] = jnp.zeros((160, 128), BF)
+        edge[:, :, 0:128] = jnp.zeros((5, 16, 128), BF)
+        edge[:, :, 1152:1280] = jnp.zeros((5, 16, 128), BF)
         for x in range(10):
-            part = rounded[x * 16:x * 16 + 16]
-            if x == 0:
-                part = part * left_ok
-            if x == 9:
-                part = part * right_ok
-            imx[x * 16:x * 16 + 16, inner] = part.astype(BF)
+            uc[x * 16:x * 16 + 16, 128:1152] = u[x + 1]
+
+        def pair(first, second):
+            return jnp.concatenate([first, second], axis=0).astype(BF)
+
+        edge[0, :, 128:1152] = pair(low_y[0:8], high_y[0:8])
+        edge[1, :, 128:1152] = pair(get_column(uf, 64 + 7), get_column(uf, 64 + 24))
+        edge[2, :, 128:1152] = pair(get_column(uf, 7), get_column(uf, 24))
+        edge[3, :, 128:1152] = pair(rows_at(0), high_y[8:16])
+        edge[4, :, 128:1152] = pair(low_y[8:16], rows_at(15))
+
+        left_ok = jnp.where(has_left, 1.0, 0.0)
+        right_ok = jnp.where(has_right, 1.0, 0.0)
+        down_ok = jnp.where(has_down, 1.0, 0.0)
+        up_ok = jnp.where(has_up, 1.0, 0.0)
+
+        def image_part(jb, _):
+            here = pl.ds(pl.multiple_of(jb * 256, 128), 256)
+            inner = pl.ds(pl.multiple_of(jb * 256 + 128, 128), 256)
+            window = pl.ds(pl.multiple_of(jb * 256, 128), 512)
+            total = dot(uc[:, window], wst[0, 0:512])
+            total += dot(u[2:12, :, here].reshape(160, 256), wst[0, 512:768])
+            total += dot(u[0:10, :, here].reshape(160, 256), wst[0, 768:1024])
+            plus = shifted(uf, jb, 9, 0, 10)
+            total += dot(plus.astype(BF), wst[0, 1024:1280])
+            minus = shifted(uf, jb, 7, 0, 10)
+            total += dot(minus.astype(BF), wst[0, 1280:1536])
+            rounded = total.astype(BF).astype(F32)
+            for x in range(10):
+                part = rounded[x * 16:x * 16 + 16]
+                if x == 0:
+                    part = part * left_ok
+                if x == 9:
+                    part = part * right_ok
+                imx[x * 16:x * 16 + 16, inner] = part.astype(BF)
+                for k in range(2):
+                    imf[2 * jb + k, x * 32 + 8:x * 32 + 24, :] = part[:, k * 128:k * 128 + 128]
+            rim = dot(edge[0, :, window], wst[0, 0:512])
+            for d in range(4):
+                rim += dot(edge[d + 1, :, inner], wst[0, 512 + d * 256:768 + d * 256])
+            rim = rim.astype(BF).astype(F32)
             for k in range(2):
-                imf[2 * jb + k, x * 32 + 8:x * 32 + 24, :] = part[:, k * 128:k * 128 + 128]
-        rim = dot(edge[0, :, window], wst[0, 0:512])
-        for d in range(4):
-            rim += dot(edge[d + 1, :, inner], wst[0, 512 + d * 256:768 + d * 256])
-        rim = rim.astype(BF).astype(F32)
-        for k in range(2):
-            lanes = slice(k * 128, k * 128 + 128)
-            imf[2 * jb + k, pl.ds(39, 8, stride=32), :] = rim[0:8, lanes] * down_ok
-            imf[2 * jb + k, pl.ds(56, 8, stride=32), :] = rim[8:16, lanes] * up_ok
-        return 0
-
-    lax.fori_loop(0, 4, image_part, 0)
-
-    def prior_part(jb, _):
-        here = pl.ds(pl.multiple_of(jb * 256, 128), 256)
-        inner = pl.ds(pl.multiple_of(jb * 256 + 128, 128), 256)
-        window = pl.ds(pl.multiple_of(jb * 256, 128), 512)
-        total = dot(imx[16:144, window], wst[1, 0:512])
-        total += dot(imx[0:128, inner], wst[1, 512:768])
-        total += dot(imx[32:160, inner], wst[1, 768:1024])
-        minus = shifted(imf, jb, 7, 1, 9)
-        total += dot(minus.astype(BF), wst[1, 1024:1280])
-        plus = shifted(imf, jb, 9, 1, 9)
-        total += dot(plus.astype(BF), wst[1, 1280:1536])
-        prior[:, here] = total
-        return 0
-
-    lax.fori_loop(0, 4, prior_part, 0)
-
-    some = gotcode.at[pl.ds(0, n - 1)]
-    remote(some, some, code_send.at[0], code_recv.at[0], (gy, right)).wait_recv()
+                lanes = slice(k * 128, k * 128 + 128)
+                imf[2 * jb + k, pl.ds(39, 8, stride=32), :] = rim[0:8, lanes] * down_ok
+                imf[2 * jb + k, pl.ds(56, 8, stride=32), :] = rim[8:16, lanes] * up_ok
+            return 0
+
+        lax.fori_loop(0, 4, image_part, 0)
+
+        def prior_part(jb, _):
+            here = pl.ds(pl.multiple_of(jb * 256, 128), 256)
+            inner = pl.ds(pl.multiple_of(jb * 256 + 128, 128), 256)
+            window = pl.ds(pl.multiple_of(jb * 256, 128), 512)
+            total = dot(imx[16:144, window], wst[1, 0:512])
+            total += dot(imx[0:128, inner], wst[1, 512:768])
+            total += dot(imx[32:160, inner], wst[1, 768:1024])
+            minus = shifted(imf, jb, 7, 1, 9)
+            total += dot(minus.astype(BF), wst[1, 1024:1280])
+            plus = shifted(imf, jb, 9, 1, 9)
+            total += dot(plus.astype(BF), wst[1, 1280:1536])
+            prior[:, here] = total
+            return 0
+
+        lax.fori_loop(0, 4, prior_part, 0)
+
+    def codes_in():
+        remote(some, some, code_send.at[0], code_recv.at[0], (gy, right)).wait_recv()
+        quarter = iota((1, 128), 1) // 32
+        rows128 = iota((128, 128), 0)
+
+        def hits(q, _):
+            key = gotcode[4 * q]
+            for o in range(1, 4):
+                key = jnp.where(quarter == o, gotcode[4 * q + o], key)
+            hit = jnp.where(rows128 == jnp.right_shift(key, 4), 1.0, 0.0).astype(BF).reshape(8, 16, 128)
+            layer = jnp.broadcast_to(jnp.bitwise_and(key, 15), (16, 128))
+            lanes = pl.ds(pl.multiple_of(q * 128, 128), 128)
+            for z in range(16):
+                only = jnp.where(layer == z, 1.0, 0.0).astype(BF)
+                hot[z % 2, z // 2 * 128:z // 2 * 128 + 128, lanes] = (hit * only).reshape(128, 128)
+            return 0
+
+        lax.fori_loop(0, n // 4, hits, 0)
+
     low_lane = iota((GROUP * 16, 128), 1) < 64
-    cell16 = iota((128, GROUP * 32), 0) * 16
-    quarter = iota((1, 128), 1) // 32
     groups = n // GROUP
-    for g in range(groups):
+
+    def take(g):
         first = g * GROUP
         arriving = GROUP if g < groups - 1 else GROUP - 1
         part = got.at[pl.ds(first, arriving)]
@@ -305,35 +323,35 @@
             (1, 1, jnp.where(low_lane, wr, hi), lo),
         ):
             at = slice(slots * 16, slots * 16 + 16)
-            rhs[parity, :, at, 0:128] = one.astype(BF).reshape(GROUP, 16, 128)
-            rhs[parity, :, at, 128:256] = two.astype(BF).reshape(GROUP, 16, 128)
-        keys = []
-        for q in range(GROUP // 4):
-            key = gotcode[first + 4 * q]
-            for o in range(1, 4):
-                key = jnp.where(quarter == o, gotcode[first + 4 * q + o], key)
-            keys.append(key)
-        key = jnp.concatenate(keys, axis=1)
-
-        def layer(zz, _, g=g, key=key):
-            for parity in range(2):
-                z = 2 * zz + parity
-                hit = jnp.where(cell16 == key - z, 1.0, 0.0).astype(BF)
-                part = dot(hit, rhs[parity].reshape(GROUP * 32, 256))
-                acc[z] = part if g == 0 else acc[z] + part
-            return 0
-
-        lax.fori_loop(0, 8, layer, 0)
+            rhs[parity, first:first + GROUP, at, 0:128] = one.astype(BF).reshape(GROUP, 16, 128)
+            rhs[parity, first:first + GROUP, at, 128:256] = two.astype(BF).reshape(GROUP, 16, 128)
+
+    def add(start, stop):
+        for parity in range(2):
+            lists = rhs[parity, start * GROUP:stop * GROUP].reshape(-1, 256)
+            part = dot(hot[parity, :, start * GROUP * 32:stop * GROUP * 32], lists)
+            acc[parity] = part if start == 0 else acc[parity] + part
+
+    some = gotcode.at[pl.ds(0, n - 1)]
+    matrices()
+    codes_in()
+    take(0)
+    beyond()
+    for g in range(1, groups - 1):
+        take(g)
+    add(0, groups - 1)
+    take(groups - 1)
+    add(groups - 1, groups)
 
     low_out = iota((128, 128), 1) < 64
     for zz in range(8):
-        even, odd = acc[2 * zz], acc[2 * zz + 1]
-        lanes = slice(zz * 128, zz * 128 + 128)
+        rows = slice(zz * 128, zz * 128 + 128)
+        even, odd = acc[0, rows], acc[1, rows]
         s1 = jnp.where(low_out, even[:, 0:128] + even[:, 128:256], odd[:, 0:128] + odd[:, 128:256])
         s0 = pltpu.roll(jnp.where(low_out, odd[:, 0:128], even[:, 0:128]), 64, 1)
-        own = u[2:10, :, lanes].astype(F32).reshape(128, 128)
-        grad = s1 - own * s0 - prior[:, lanes]
-        res[:, :, lanes] = grad.astype(BF).reshape(8, 16, 128)
+        own = u[2:10, :, rows].astype(F32).reshape(128, 128)
+        grad = s1 - own * s0 - prior[:, rows]
+        res[:, :, rows] = grad.astype(BF).reshape(8, 16, 128)
 
     put = pltpu.make_async_copy(res, out, out_sem.at[0])
     put.start()
@@ -352,8 +370,8 @@
     return pl.pallas_call(
         functools.partial(kernel, n, m),
         out_shape=jax.ShapeDtypeStruct(field.shape, BF),
-        in_specs=[pl.BlockSpec(memory_space=pl.ANY)] * 7,
-        out_specs=pl.BlockSpec(memory_space=pl.ANY),
+        in_specs=[pl.BlockSpec(memory_space=pltpu.HBM)] * 7,
+        out_specs=pl.BlockSpec(memory_space=pltpu.HBM),
         scratch_shapes=[
             vm((12, 16, 1024), BF),
             vm((n, 2048), BF),
@@ -378,14 +396,15 @@
             vm((160, 1280), BF),
             vm((2, 1536, 256), BF),
             vm((128, 1024), F32),
-            vm((2, GROUP, 32, 256), BF),
-            vm((16, 128, 256), F32),
+            vm((2, n, 32, 256), BF),
+            vm((2, 1024, n * 32), BF),
+            vm((2, 1024, 256), F32),
             vm((8, 16, 1024), BF),
             dma((7,)), dma((1,)), dma((8,)), dma((8,)),
             dma((1,)), dma((n // GROUP,)), dma((1,)), dma((1,)),
         ],
         compiler_params=pltpu.CompilerParams(
-            collective_id=0, has_side_effects=True, vmem_limit_bytes=40 * 1024 * 1024
+            collective_id=0, has_side_effects=True, vmem_limit_bytes=56 * 1024 * 1024
         ),
     )(
         field, center_block, couple_blocks, cell_index.reshape(n, 32),

time: 51.7 us -> 42.5 us (0.82)
  the two profiles are of different devices: /device:TPU:1 before, /device:TPU:39 now
where the time goes in v2:
time: 42.5 us; the launch traced here: 42.3 us
  Pallas kernels  40.6 us (96%)
  local copies, waits for them, and re-layouts  1.67 us (4%)
    pallas_call x1, Pallas kernels, on_device(): pl.pallas_call(functools.partial(kernel, n, m), out_shape=jax.ShapeDtypeS...  40.6 us
    unnamed x1, local copies, waits for them, and re-layouts  1.67 us

profile of v2, /device:TPU:39, one launch (start us, length us, event | category | flops | bytes accessed | tf_op | source)
XLA Modules:
  0.0 42.3 jit_solution(17635152035088051436)
XLA Ops:
  0.0 40.6 %shard_map.73 = bf16[8,16,1024]{2,1,0:T(8,128)(2,1)} custom-call(bf16[8,16,1024]{2,1,0:T(8,128)(2,1)} %field.1, bf16[64,64]{1,0:T(8,128)(2,1)} %center.1, bf16[6,64,64]{2,1,0:T(8,128)(2,1)} %couple.1, s32[32,32]{1,0:T(8,128)} %bitcast.6, s32[1,32]{1,0:T(1,128)} %bitcast.7, bf16[32,2048]{1,0:T(8,128)(2,1)} %bitcast.4, bf16[32,2048]{1,0:T(8,128)(2,1)} %bitcast.5), custom_call_target="tpu_custom_call" | custom-call | tf_op jit(solution)/shard_map/pallas_call | solution.py:370
  40.6 1.7 %copy.9 = bf16[8,16,1024]{2,1,0:T(8,128)(2,1)} copy(bf16[8,16,1024]{2,1,0:T(8,128)(2,1)} %shard_map.73) | data formatting | bytes 524288

commit v3 on v2

--- a/solution.py
+++ b/solution.py
@@ -10,7 +10,8 @@
 BF = jnp.bfloat16
 F32 = jnp.float32
 MESH = pl.DeviceIdType.MESH
-GROUP = 8
+SENT = (0, 1, 3, 2)
+ZS = 4
 
 
 def dot(a, b):
@@ -78,6 +79,7 @@
     for one in ins:
         one.start()
 
+    size = n // ZS
     barrier = pltpu.get_barrier_semaphore()
 
     def greet(d, _):
@@ -87,8 +89,19 @@
         return 0
 
     lax.fori_loop(1, n, greet, 0)
-    for who in ((down, gx), (up, gx), (down, left), (down, right), (up, left), (up, right)):
-        pl.semaphore_signal(barrier, inc=1, device_id=who, device_id_type=MESH)
+    has_left, has_right, has_down, has_up = gx > 0, gx < n - 1, gy > 0, gy < m - 1
+    beside = (
+        (has_down, (down, gx)), (has_up, (up, gx)),
+        (has_down & has_left, (down, left)), (has_down & has_right, (down, right)),
+        (has_up & has_left, (up, left)), (has_up & has_right, (up, right)),
+    )
+    greetings = n - 1
+    for there, who in beside:
+        greetings += jnp.where(there, 1, 0)
+
+        @pl.when(there)
+        def _(who=who):
+            pl.semaphore_signal(barrier, inc=1, device_id=who, device_id_type=MESH)
 
     for which, (copy, src) in enumerate(((ins[0], av), (ins[1], wv))):
         copy.wait()
@@ -126,7 +139,7 @@
         for j in range(8):
             csend[c, j:j + 1, :] = uf[j, place:place + 1, :]
 
-    pl.semaphore_wait(barrier, n - 1 + 6)
+    pl.semaphore_wait(barrier, greetings)
 
     def remote(src, dst, send, recv, who):
         return pltpu.make_async_remote_copy(
@@ -135,35 +148,49 @@
         )
 
     halos = [
-        remote(u.at[pl.ds(2, 2)], u.at[pl.ds(10, 2)], halo_send.at[0], halo_recv.at[0], (gy, left)),
-        remote(u.at[pl.ds(8, 2)], u.at[pl.ds(0, 2)], halo_send.at[1], halo_recv.at[1], (gy, right)),
-        remote(ysend.at[0], yrecv.at[1], halo_send.at[2], halo_recv.at[2], (down, gx)),
-        remote(ysend.at[1], yrecv.at[0], halo_send.at[3], halo_recv.at[3], (up, gx)),
-        remote(csend.at[0], crecv.at[0], halo_send.at[4], halo_recv.at[4], (up, right)),
-        remote(csend.at[1], crecv.at[1], halo_send.at[5], halo_recv.at[5], (down, right)),
-        remote(csend.at[2], crecv.at[2], halo_send.at[6], halo_recv.at[6], (up, left)),
-        remote(csend.at[3], crecv.at[3], halo_send.at[7], halo_recv.at[7], (down, left)),
+        (has_left, has_right, u.at[pl.ds(2, 2)], u.at[pl.ds(10, 2)], (gy, left)),
+        (has_right, has_left, u.at[pl.ds(8, 2)], u.at[pl.ds(0, 2)], (gy, right)),
+        (has_down, has_up, ysend.at[0], yrecv.at[1], (down, gx)),
+        (has_up, has_down, ysend.at[1], yrecv.at[0], (up, gx)),
+        (has_up & has_right, has_down & has_left, csend.at[0], crecv.at[0], (up, right)),
+        (has_down & has_right, has_up & has_left, csend.at[1], crecv.at[1], (down, right)),
+        (has_up & has_left, has_down & has_right, csend.at[2], crecv.at[2], (up, left)),
+        (has_down & has_left, has_up & has_right, csend.at[3], crecv.at[3], (down, left)),
     ]
-    for one in halos:
-        one.start()
-
-    def send_code(d, _):
-        to = lax.rem(gx + d, n)
-        remote(code.at[to], gotcode.at[d - 1], code_send.at[0], code_recv.at[0], (gy, to)).start()
-        return 0
-
-    lax.fori_loop(1, n, send_code, 0)
-
-    def send_list(d, _):
-        to = lax.rem(gx + d, n)
-        remote(
-            msg.at[to], got.at[d - 1], list_send.at[0], list_recv.at[(d - 1) // GROUP], (gy, to)
-        ).start()
-        return 0
-
-    lax.fori_loop(1, n, send_list, 0)
-    got[n - 1] = msg[gx]
-    gotcode[n - 1] = code[gx]
+
+    def halo(k, what):
+        sends, receives, src, dst, who = halos[k]
+        copy = remote(src, dst, halo_send.at[k], halo_recv.at[k], who)
+
+        @pl.when(receives if what == "wait_recv" else sends)
+        def _():
+            getattr(copy, what)()
+
+    for k in range(8):
+        halo(k, "start")
+
+    def partner(g, k):
+        y, z, c = gx // 8 + k // 2, lax.rem(gx // 2, ZS) + g, lax.rem(gx, 2) + lax.rem(k, 2)
+        return lax.rem(y, n // 8) * 8 + lax.rem(z, ZS) * 2 + lax.rem(c, 2)
+
+    def send_code(g, k):
+        to = partner(g, k)
+        remote(code.at[to], gotcode.at[g * size + k], code_send.at[0], code_recv.at[0], (gy, to)).start()
+
+    def send_list(g, k):
+        to = partner(g, k)
+        remote(msg.at[to], got.at[g * size + k], list_send.at[0], list_recv.at[g], (gy, to)).start()
+
+    for send in (send_code, send_list):
+        for g in SENT:
+
+            def each(k, _, g=g, send=send):
+                send(g, k)
+                return 0
+
+            lax.fori_loop(1 if g == 0 else 0, size, each, 0)
+    got[0] = msg[gx]
+    gotcode[0] = code[gx]
 
     def matrices():
         ins[5].wait()
@@ -191,9 +218,8 @@
                 ).astype(BF)
 
     def beyond():
-        has_left, has_right, has_down, has_up = gx > 0, gx < n - 1, gy > 0, gy < m - 1
-        for one in halos:
-            one.wait_recv()
+        for k in range(8):
+            halo(k, "wait_recv")
         zero = jnp.zeros((), F32)
         for slot, ok in ((0, has_left), (10, has_right)):
             for x in (slot, slot + 1):
@@ -302,16 +328,14 @@
 
         lax.fori_loop(0, n // 4, hits, 0)
 
-    low_lane = iota((GROUP * 16, 128), 1) < 64
-    groups = n // GROUP
+    low_lane = iota((size * 16, 128), 1) < 64
 
     def take(g):
-        first = g * GROUP
-        arriving = GROUP if g < groups - 1 else GROUP - 1
-        part = got.at[pl.ds(first, arriving)]
+        first = g * size
+        part = got.at[pl.ds(first, size)] if g else got.at[pl.ds(1, size - 1)]
         remote(part, part, list_send.at[0], list_recv.at[g], (gy, right)).wait_recv()
-        a = got[first:first + GROUP, 0:16, :].astype(F32).reshape(GROUP * 16, 128)
-        w = got[first:first + GROUP, 16:32, :].astype(F32).reshape(GROUP * 16, 128)
+        a = got[first:first + size, 0:16, :].astype(F32).reshape(size * 16, 128)
+        w = got[first:first + size, 16:32, :].astype(F32).reshape(size * 16, 128)
         p = a * w
         hi = p.astype(BF).astype(F32)
         lo = p - hi
@@ -323,27 +347,27 @@
             (1, 1, jnp.where(low_lane, wr, hi), lo),
         ):
             at = slice(slots * 16, slots * 16 + 16)
-            rhs[parity, first:first + GROUP, at, 0:128] = one.astype(BF).reshape(GROUP, 16, 128)
-            rhs[parity, first:first + GROUP, at, 128:256] = two.astype(BF).reshape(GROUP, 16, 128)
+            rhs[parity, first:first + size, at, 0:128] = one.astype(BF).reshape(size, 16, 128)
+            rhs[parity, first:first + size, at, 128:256] = two.astype(BF).reshape(size, 16, 128)
 
     def add(start, stop):
         for parity in range(2):
-            lists = rhs[parity, start * GROUP:stop * GROUP].reshape(-1, 256)
-            part = dot(hot[parity, :, start * GROUP * 32:stop * GROUP * 32], lists)
+            lists = rhs[parity, start * size:stop * size].reshape(-1, 256)
+            part = dot(hot[parity, :, start * size * 32:stop * size * 32], lists)
             acc[parity] = part if start == 0 else acc[parity] + part
 
-    some = gotcode.at[pl.ds(0, n - 1)]
+    some = gotcode.at[pl.ds(1, n - 1)]
     matrices()
     codes_in()
     take(0)
     beyond()
-    for g in range(1, groups - 1):
-        take(g)
-    add(0, groups - 1)
-    take(groups - 1)
-    add(groups - 1, groups)
+    take(1)
+    take(3)
+    take(2)
+    add(0, ZS)
 
     low_out = iota((128, 128), 1) < 64
+    puts = []
     for zz in range(8):
         rows = slice(zz * 128, zz * 128 + 128)
         even, odd = acc[0, rows], acc[1, rows]
@@ -352,15 +376,21 @@
         own = u[2:10, :, rows].astype(F32).reshape(128, 128)
         grad = s1 - own * s0 - prior[:, rows]
         res[:, :, rows] = grad.astype(BF).reshape(8, 16, 128)
-
-    put = pltpu.make_async_copy(res, out, out_sem.at[0])
-    put.start()
-    for one in halos:
-        one.wait_send()
+        if zz % 2:
+            put = pltpu.make_async_copy(
+                res.at[:, :, pl.ds(zz * 128 - 128, 256)], out.at[:, :, pl.ds(zz * 128 - 128, 256)],
+                out_sem.at[zz // 2],
+            )
+            put.start()
+            puts.append(put)
+
+    for k in range(8):
+        halo(k, "wait_send")
     remote(some, some, code_send.at[0], code_recv.at[0], (gy, right)).wait_send()
-    every = got.at[pl.ds(0, n - 1)]
+    every = got.at[pl.ds(1, n - 1)]
     remote(every, every, list_send.at[0], list_recv.at[0], (gy, right)).wait_send()
-    put.wait()
+    for put in puts:
+        put.wait()
 
 
 def on_device(field, center_block, couple_blocks, cell_index, slot_counts, assays, assay_weights):
@@ -400,8 +430,8 @@
             vm((2, 1024, n * 32), BF),
             vm((2, 1024, 256), F32),
             vm((8, 16, 1024), BF),
-            dma((7,)), dma((1,)), dma((8,)), dma((8,)),
-            dma((1,)), dma((n // GROUP,)), dma((1,)), dma((1,)),
+            dma((7,)), dma((4,)), dma((8,)), dma((8,)),
+            dma((1,)), dma((ZS,)), dma((1,)), dma((1,)),
         ],
         compiler_params=pltpu.CompilerParams(
             collective_id=0, has_side_effects=True, vmem_limit_bytes=56 * 1024 * 1024

time: 42.5 us -> 40.8 us (0.960)
  Pallas kernels: 40.6 us -> 39 us
    pallas_call x1, Pallas kernels: 40.6 us -> 39 us  [on_device(): pl.pallas_call(functools.partial(kernel, n, m), out_shape=jax.ShapeDtypeS...]
where the time goes in v3:
time: 40.8 us; the launch traced here: 40.6 us
  Pallas kernels  39 us (96%)
  local copies, waits for them, and re-layouts  1.67 us (4%)
    pallas_call x1, Pallas kernels, on_device(): pl.pallas_call(functools.partial(kernel, n, m), out_shape=jax.ShapeDtypeS...  39 us
    unnamed x1, local copies, waits for them, and re-layouts  1.67 us

profile of v3, /device:TPU:39, one launch (start us, length us, event | category | flops | bytes accessed | tf_op | source)
XLA Modules:
  0.0 40.6 jit_solution(4079351222173521185)
XLA Ops:
  0.0 39.0 %shard_map.73 = bf16[8,16,1024]{2,1,0:T(8,128)(2,1)} custom-call(bf16[8,16,1024]{2,1,0:T(8,128)(2,1)} %field.1, bf16[64,64]{1,0:T(8,128)(2,1)} %center.1, bf16[6,64,64]{2,1,0:T(8,128)(2,1)} %couple.1, s32[32,32]{1,0:T(8,128)} %bitcast.6, s32[1,32]{1,0:T(1,128)} %bitcast.7, bf16[32,2048]{1,0:T(8,128)(2,1)} %bitcast.4, bf16[32,2048]{1,0:T(8,128)(2,1)} %bitcast.5), custom_call_target="tpu_custom_call" | custom-call | tf_op jit(solution)/shard_map/pallas_call | solution.py:400
  39.0 1.7 %copy.9 = bf16[8,16,1024]{2,1,0:T(8,128)(2,1)} copy(bf16[8,16,1024]{2,1,0:T(8,128)(2,1)} %shard_map.73) | data formatting | bytes 524288

commit v4 on v3

--- a/solution.py
+++ b/solution.py
@@ -107,7 +107,7 @@
         copy.wait()
         for j in range(16):
             stage[pl.ds(j, n, stride=16), :] = src[:, j * 128:(j + 1) * 128].astype(F32)
-        msg[:, which * 16:(which + 1) * 16, :] = stage[...].reshape(n, 16, 128).astype(BF)
+        msg[:, which * 16:(which + 1) * 16, :] = stage[0:n * 16, :].reshape(n, 16, 128).astype(BF)
 
     ins[3].wait()
     ins[4].wait()
@@ -410,7 +410,7 @@
             vm((1, n), i32),
             vm((64, 64), BF),
             vm((6, 64, 64), BF),
-            vm((n * 16, 128), F32),
+            vm((n * 16 + 16, 128), F32),
             vm((n, 32, 128), BF),
             vm((n, 32, 128), BF),
             vm((n, 1, 128), i32),
@@ -419,10 +419,10 @@
             vm((2, 16, 1024), BF),
             vm((4, 8, 128), F32),
             vm((4, 8, 128), F32),
-            vm((8, 320, 128), F32),
+            vm((8, 384, 128), F32),
             vm((160, 1280), BF),
             vm((5, 16, 1280), BF),
-            vm((8, 320, 128), F32),
+            vm((8, 384, 128), F32),
             vm((160, 1280), BF),
             vm((2, 1536, 256), BF),
             vm((128, 1024), F32),

time: 40.8 us -> 40.8 us (level)
  no operation moved by 1% of the time
where the time goes in v4:
time: 40.8 us; the launch traced here: 40.6 us
  Pallas kernels  39 us (96%)
  local copies, waits for them, and re-layouts  1.67 us (4%)
    pallas_call x1, Pallas kernels, on_device(): pl.pallas_call(functools.partial(kernel, n, m), out_shape=jax.ShapeDtypeS...  39 us
    unnamed x1, local copies, waits for them, and re-layouts  1.67 us

profile of v4, /device:TPU:39, one launch (start us, length us, event | category | flops | bytes accessed | tf_op | source)
XLA Modules:
  0.0 40.6 jit_solution(931195871983908890)
XLA Ops:
  0.0 39.0 %shard_map.73 = bf16[8,16,1024]{2,1,0:T(8,128)(2,1)} custom-call(bf16[8,16,1024]{2,1,0:T(8,128)(2,1)} %field.1, bf16[64,64]{1,0:T(8,128)(2,1)} %center.1, bf16[6,64,64]{2,1,0:T(8,128)(2,1)} %couple.1, s32[32,32]{1,0:T(8,128)} %bitcast.6, s32[1,32]{1,0:T(1,128)} %bitcast.7, bf16[32,2048]{1,0:T(8,128)(2,1)} %bitcast.4, bf16[32,2048]{1,0:T(8,128)(2,1)} %bitcast.5), custom_call_target="tpu_custom_call" | custom-call | tf_op jit(solution)/shard_map/pallas_call | solution.py:400
  39.0 1.7 %copy.9 = bf16[8,16,1024]{2,1,0:T(8,128)(2,1)} copy(bf16[8,16,1024]{2,1,0:T(8,128)(2,1)} %shard_map.73) | data formatting | bytes 524288
